TPU v7x, 256 devices: a whole 4x4x8 slice. The times are simulated.
256 devices in a mesh: query: 32 (over x, z_hi, y), entity: 8 (over z_lo, core).
Axes of the slice: x: 4, y: 4, z: 8 (z_hi: 2, z_lo: 4; z = z_hi * 4 + z_lo), core: 2. Of those that a mesh axis runs over, the one named last changes fastest.
Arguments:
- anchor_ids: int32 [16384], P('query'), may hold values from 0 to 32767
- relation_ids: int32 [16384], P('query'), may hold values from 0 to 4130
- side_flags: int32 [16384], P('query'), may hold values from 0 to 1
- teacher_entities: bfloat16 [32768, 1000], P(('entity', 'query')), may hold values from -1.2 to 1.2, as said below
- student_entities: bfloat16 [32768, 128], P(('entity', 'query')), may hold values from -2.1 to 2.1, as said below
- teacher_relations: bfloat16 [4131, 1000], replicated, may hold values from -9 to 33, as said below
- student_relations: bfloat16 [4131, 128], replicated, may hold values from -9 to 63.6875, as said below
Outputs:
- divergence: float32 [16384], P('query')
- entity_grad: float32 [32768, 128], P(('entity', 'query'))
- query_grad: float32 [16384, 128], P('query')
Inputs may be any that keep to these rules, and one draw needn't show every extreme that they name: `teacher_entities`: Real-valued embeddings. `student_entities`: Real-valued embeddings. `teacher_relations`: Real-valued embeddings. `student_relations`: Real-valued embeddings.
All inputs are finite; a program needn't handle non-finite values.
Results may differ from a plain program's by a relative error of at most 0.013.
Values may be sent and summed in bfloat16 or wider, within the bound.
A program may use at most 128 MiB of HBM per device.

v0:
```python
import jax
import jax.numpy as jnp
from jax import lax
from jax.sharding import PartitionSpec as P


def query_vectors(anchor, relation, flags):
    half = anchor.shape[1] // 2
    sign = (2 * flags - 1).astype(jnp.float32)[:, None]
    a_re = anchor[:, :half]
    a_im = anchor[:, half:]
    r_re = relation[:, :half]
    r_im = relation[:, half:]
    real = a_re * r_re - sign * a_im * r_im
    imag = a_im * r_re + sign * a_re * r_im
    return jnp.concatenate([real, imag], axis=1).astype(jnp.bfloat16)


def per_device(
    anchor_ids,
    relation_ids,
    side_flags,
    teacher_entities,
    student_entities,
    teacher_relations,
    student_relations,
):
    teacher_slab, student_slab = (
        lax.all_gather(teacher_entities, "query", axis=0, tiled=True),
        lax.all_gather(student_entities, "query", axis=0, tiled=True),
    )
    slab = teacher_slab.shape[0]
    offset = lax.axis_index("entity") * slab
    local = anchor_ids - offset
    inside = ((local >= 0) & (local < slab))[:, None]
    safe = jnp.clip(local, 0, slab - 1)
    teacher_part = jnp.where(inside, jnp.take(teacher_slab, safe, axis=0).astype(jnp.float32), 0.0)
    student_part = jnp.where(inside, jnp.take(student_slab, safe, axis=0).astype(jnp.float32), 0.0)
    teacher_anchor, student_anchor = (
        lax.psum(teacher_part.astype(jnp.bfloat16), "entity").astype(jnp.float32),
        lax.psum(student_part.astype(jnp.bfloat16), "entity").astype(jnp.float32),
    )
    query_teacher = query_vectors(
        teacher_anchor,
        jnp.take(teacher_relations, relation_ids, axis=0).astype(jnp.float32),
        side_flags,
    )
    query_student = query_vectors(
        student_anchor,
        jnp.take(student_relations, relation_ids, axis=0).astype(jnp.float32),
        side_flags,
    )
    rows = query_teacher.shape[0]
    block = 1024
    count = slab // block
    teacher_blocks = teacher_slab.reshape(count, block, teacher_slab.shape[1])
    student_blocks = student_slab.reshape(count, block, student_slab.shape[1])

    def first_pass(carry, items):
        top_t, total_t, weighted, top_s, total_s = carry
        t = jnp.dot(query_teacher, items[0].T, preferred_element_type=jnp.float32)
        s = jnp.dot(query_student, items[1].T, preferred_element_type=jnp.float32)
        new_t = jnp.maximum(top_t, jnp.max(t, axis=1))
        factor_t = jnp.exp(top_t - new_t)
        expo_t = jnp.exp(t - new_t[:, None])
        total_t = total_t * factor_t + jnp.sum(expo_t, axis=1)
        weighted = weighted * factor_t + jnp.sum(expo_t * (t - s), axis=1)
        new_s = jnp.maximum(top_s, jnp.max(s, axis=1))
        total_s = total_s * jnp.exp(top_s - new_s) + jnp.sum(jnp.exp(s - new_s[:, None]), axis=1)
        kept = None
        return ((new_t, total_t, weighted, new_s, total_s), kept)

    lowest = jnp.full((rows,), -jnp.inf, jnp.float32)
    nothing = jnp.zeros((rows,), jnp.float32)
    stats, kept = lax.scan(
        first_pass, (lowest, nothing, nothing, lowest, nothing), (teacher_blocks, student_blocks)
    )
    top_t, total_t, weighted, top_s, total_s = stats
    best_t, best_s = lax.pmax((top_t, top_s), "entity")
    factor_t = jnp.exp(top_t - best_t)
    factor_s = jnp.exp(top_s - best_s)
    total_t, weighted, total_s = lax.psum(
        (total_t * factor_t, weighted * factor_t, total_s * factor_s), "entity"
    )
    top_t, top_s = (best_t, best_s)
    divergence = weighted / total_t - top_t - jnp.log(total_t) + top_s + jnp.log(total_s)

    def second_pass(q_grad, items):
        t = jnp.dot(query_teacher, items[0].T, preferred_element_type=jnp.float32)
        s = jnp.dot(query_student, items[1].T, preferred_element_type=jnp.float32)
        prob_t = jnp.exp(t - top_t[:, None]) / total_t[:, None]
        prob_s = jnp.exp(s - top_s[:, None]) / total_s[:, None]
        weights = (prob_s - prob_t).astype(jnp.bfloat16)
        grad_block = jnp.dot(weights.T, query_student, preferred_element_type=jnp.float32)
        q_grad = q_grad + jnp.dot(weights, items[1], preferred_element_type=jnp.float32)
        return (q_grad, grad_block)

    start = jnp.zeros((rows, query_student.shape[1]), jnp.float32)
    q_grad, grad_blocks = lax.scan(second_pass, start, (teacher_blocks, student_blocks))
    slab_grad = grad_blocks.reshape(slab, query_student.shape[1])
    entity_grad = lax.psum_scatter(slab_grad, "query", scatter_dimension=0, tiled=True)
    query_grad = lax.psum(q_grad, "entity")
    return (divergence, entity_grad, query_grad)


def solution(mesh):
    in_specs = (
        P("query"),
        P("query"),
        P("query"),
        P(("entity", "query"), None),
        P(("entity", "query"), None),
        P(),
        P(),
    )
    out_specs = (P("query"), P(("entity", "query"), None), P("query", None))
    return jax.shard_map(
        per_device, mesh=mesh, in_specs=in_specs, out_specs=out_specs, check_vma=False
    )
```

profile of v0, /device:TPU:32, one launch (start us, length us, event | category | flops | bytes accessed | tf_op | source)
XLA Modules:
  0.0 744.2 jit_solution(13715478936245018552)
XLA Ops:
  7.2 0.7 all-gather.5.cloned.1.call-update
  8.0 1.8 copy.10
  9.9 0.7 compare_and_fusion.1
  10.6 83.7 %all-gather.5.cloned.1.call-done = bf16[4096,128]{1,0:T(8,128)(2,1)} async-done(((bf16[128,128]{1,0:T(8,128)(2,1)}), bf16[4096,128]{1,0:T(8,128)(2,1)}) %all-gather.5.cloned.1.call-update) | async-done | bytes 1048592 | tf_op jit(solution)/shard_map/all_gather | solution.py:30
  94.3 2.4 gather_fusion.2
  96.7 0.9 select_convert_fusion.2
  97.5 149.9 %all-gather.3.cloned.1.call-done = bf16[4096,1000]{1,0:T(8,128)(2,1)} async-done(((bf16[128,1000]{1,0:T(8,128)(2,1)}), bf16[4096,1000]{1,0:T(8,128)(2,1)}) %all-gather.3.cloned.1.call-update) | async-done | bytes 8192016 | tf_op jit(solution)/shard_map/all_gather | solution.py:29
  247.4 7.2 gather_fusion
  254.6 1.3 select_convert_fusion
  256.1 12.1 %copy.11 = bf16[4131,1000]{1,0:T(8,128)(2,1)} copy(bf16[4131,1000]{0,1:T(8,128)(2,1)} %param.16) | data formatting | bytes 16524000 | tf_op args[5]
  268.3 8.0 %gather_fusion.1 = bf16[512,1000]{1,0:T(8,128)(2,1)} fusion(bf16[4131,1000]{1,0:T(8,128)(2,1)} %copy.11, s32[1024]{0:T(1024)S(1)} %pad_clamp_fusion), kind=kCustom, calls=%fused_computation.1 | custom fusion | bytes 2050048 | tf_op jit(solution)/shard_map/jit(_take)/gather | solution.py:45
  276.3 1.3 gather_fusion.3
  277.7 0.6 add_convert_fusion.2
  278.3 0.8 select_convert_fusion.3
  279.1 1.4 select_convert_fusion.1
  280.6 43.3 %all-reduce.8.cloned.1.call-done = (bf16[512,1000]{1,0:T(8,128)(2,1)}, bf16[512,128]{1,0:T(8,128)(2,1)}) async-done(((bf16[512,1000]{1,0:T(8,128)(2,1)}, bf16[512,128]{1,0:T(8,128)(2,1)}), (bf16[512,1000]{1,0:T(8,128)(2,1)}, bf16[512,128]{1,0:T(8,128)(2,1)})) %all-reduce.8.cloned.1.call-update) | async-done | bytes 1155088 | tf_op jit(solution)/shard_map/psum | solution.py:40
  323.9 1.5 convert_element_type.33
  325.4 1.0 subtract_convert_fusion.1
  326.4 1.3 pad_maximum_fusion
  328.1 46.0 %while.32 = (s32[]{:T(128)}, f32[512]{0:T(512)S(1)}, f32[512]{0:T(512)}, f32[512]{0:T(512)}, f32[512]{0:T(512)}, /*index=5*/f32[512]{0:T(512)}, bf16[4,1024,1000...) while((s32[]{:T(128)}, f32[512]{0:T(512)S(1)}, ...), condition=%wide.region_8.9_spmd.clone, body=%wide.region_2.8_spmd.clone.sunk | while | flops 1187518464 | bytes 12046677 | solution.py:75
  328.1 5.1 fusion.51
  333.2 2.0 fusion.52
  335.2 0.7 select_maximum_fusion.4
  335.9 0.7 select_maximum_fusion.5
  336.6 2.4 multiply_reduce_fusion.2
  339.0 0.6 copy.31
  339.6 5.1 fusion.51
  344.7 2.0 fusion.52
  346.7 0.7 select_maximum_fusion.4
  347.4 0.7 select_maximum_fusion.5
  348.1 2.4 multiply_reduce_fusion.2
  350.6 0.6 copy.31
  351.2 5.1 fusion.51
  356.2 2.0 fusion.52
  358.2 0.7 select_maximum_fusion.4
  358.9 0.7 select_maximum_fusion.5
  359.6 2.4 multiply_reduce_fusion.2
  362.1 0.6 copy.31
  362.7 5.1 fusion.51
  367.7 2.0 fusion.52
  369.7 0.7 select_maximum_fusion.4
  370.4 0.7 select_maximum_fusion.5
  371.1 2.4 multiply_reduce_fusion.2
  374.2 14.8 %all-reduce.1 = (f32[512]{0:T(512)}, f32[512]{0:T(512)}) all-reduce(f32[512]{0:T(512)} %get-tuple-element.120, f32[512]{0:T(512)S(1)} %get-tuple-element.118), channel_id=1, replica_groups=mesh['query'=32,'entity'=8] {'entity'}, use_global_device_ids=true, to_apply=%region_12.13 | all-reduce | flops 1024 | bytes 8192 | tf_op jit(solution)/shard_map/pmax | solution.py:79
  389.0 0.7 fusion.24
  389.7 14.6 %all-reduce = (f32[512]{0:T(512)S(1)}, f32[512]{0:T(512)}, f32[512]{0:T(512)}) all-reduce(f32[512]{0:T(512)S(1)} %get-tuple-element.261, f32[512]{0:T(512)S(1)} %get-tuple-element.259, f32[512]{0:T(512)S(1)} %get-tuple-element.258), channel_id=1, replica_groups=mesh['query'=32,'entity'=8] {'entity'}, use_global_device_ids=true, to_apply=%region_13.14 | all-reduce | flops 1536 | bytes 12288 | tf_op jit(solution)/shard_map/psum | solution.py:82
  404.3 26.0 %while.33 = (s32[]{:T(128)}, f32[512,128]{1,0:T(8,128)S(1)}, f32[4,1024,128]{2,1,0:T(8,128)}, bf16[4,1024,128]{2,1,0:T(8,128)(2,1)}, bf16[512,128]{1,0:T(8,128)(...) while((s32[]{:T(128)}, f32[512,128]{1,0:T(8,128)S(1)}, ...), condition=%wide.region_15.16_spmd.clone, body=%wide.region_14.15_spmd.clone.sunk | while | flops 1454505984 | bytes 16531671 | solution.py:99
  404.3 3.2 fusion.62
  407.6 1.5 subtract_convert_fusion.4
  409.6 1.2 fusion.63
  410.8 3.2 fusion.62
  414.1 1.5 subtract_convert_fusion.4
  416.1 1.2 fusion.63
  417.3 3.2 fusion.62
  420.6 1.5 subtract_convert_fusion.4
  422.6 1.2 fusion.63
  423.8 3.2 fusion.62
  427.1 1.5 subtract_convert_fusion.4
  429.1 1.2 fusion.63
  430.3 0.7 copy-done.2
  431.6 1.3 log_add_fusion
  432.9 69.5 %all-reduce.6.cloned.1.call-done = f32[512,128]{1,0:T(8,128)} async-done(((f32[512,128]{1,0:T(8,128)}), f32[512,128]{1,0:T(8,128)}) %all-reduce.6.cloned.1.call-update) | async-done | bytes 262160 | tf_op jit(solution)/shard_map/psum | solution.py:102
  502.4 233.6 %reduce-scatter.2.cloned.1.call-done = f32[128,128]{1,0:T(8,128)} async-done(((f32[4096,128]{1,0:T(8,128)}), f32[128,128]{1,0:T(8,128)}) %reduce-scatter.2.cloned.1.call-update) | async-done | bytes 65552 | tf_op jit(solution)/shard_map/reduce_scatter | solution.py:101
  736.0 1.7 copy.43
  (125 shorter events, 4.1 us)
Async XLA Ops:
  7.2 269.1 %copy-start = (bf16[4131,128]{1,0:T(8,128)(2,1)S(1)}, bf16[4131,128]{1,0:T(8,128)(2,1)}, u32[]{:S(2)}) copy-start(bf16[4131,128]{1,0:T(8,128)(2,1)} %param.17) | copy-start | bytes 3172612
  7.2 87.1 %all-gather.5.cloned.1.call-start = ((), (), s32[]{:S(2)}) async-start(), calls=%async_computation.2 | async-start | bytes 1081344 | tf_op jit(solution)/shard_map/all_gather | solution.py:30
  7.9 239.5 %all-gather.3.cloned.1.call-start = ((), (), s32[]{:S(2)}) async-start(), calls=%async_computation.1 | async-start | bytes 8650752 | tf_op jit(solution)/shard_map/all_gather | solution.py:29
  9.8 314.0 %all-reduce.8.cloned.1.call-start = ((), (), s32[]{:S(2)}) async-start(), calls=%async_computation.5 | async-start | bytes 2359296 | tf_op jit(solution)/shard_map/psum | solution.py:40
  254.6 1.4 copy-start.13
  256.0 246.4 %all-reduce.6.cloned.1.call-start = ((), (), s32[]{:S(2)}) async-start(), calls=%async_computation.4 | async-start | bytes 524288 | tf_op jit(solution)/shard_map/psum | solution.py:102
  268.3 9.4 %copy-start.14 = (s32[512]{0:T(512)S(1)}, s32[512]{0:T(512)}, u32[]{:S(2)}) copy-start(s32[512]{0:T(512)} %param.13) | copy-start | bytes 6148
  323.9 1.5 copy-start.5
  323.9 1.5 copy-start.12
  326.4 1.3 copy-start.3
  336.5 2.4 copy-start.4
  336.5 2.4 copy-start.6
  336.5 2.4 copy-start.8
  336.6 2.4 copy-start.10
  339.0 0.6 copy-start.7
  339.0 0.6 copy-start.9
  339.0 0.6 copy-start.11
  348.1 2.4 copy-start.4
  348.1 2.4 copy-start.6
  348.1 2.4 copy-start.8
  348.1 2.4 copy-start.10
  350.5 0.6 copy-start.7
  350.5 0.6 copy-start.9
  350.5 0.6 copy-start.11
  359.6 2.4 copy-start.4
  359.6 2.4 copy-start.6
  359.6 2.4 copy-start.8
  359.6 2.4 copy-start.10
  362.0 0.6 copy-start.7
  362.0 0.6 copy-start.9
  362.0 0.6 copy-start.11
  371.1 2.4 copy-start.4
  371.1 2.4 copy-start.6
  371.1 2.4 copy-start.8
  371.1 2.4 copy-start.10
  373.5 0.6 copy-start.7
  373.5 0.6 copy-start.9
  373.5 0.6 copy-start.11
  404.3 3.2 copy-start.1
  404.3 3.2 copy-start.15
  410.8 3.2 copy-start.1
  410.8 3.2 copy-start.15
  417.3 3.2 copy-start.1
  417.3 3.2 copy-start.15
  423.8 3.2 copy-start.1
  423.8 3.2 copy-start.15
  430.3 0.7 copy-start.2
  430.3 1.3 copy-start.16
  430.3 1.3 copy-start.17
  431.0 305.0 %reduce-scatter.2.cloned.1.call-start = ((), (), s32[]{:S(2)}) async-start(), calls=%async_computation.3 | async-start | bytes 2162688 | tf_op jit(solution)/shard_map/reduce_scatter | solution.py:101
Sparse Core Ops, SparseCore 0:
  11.4 82.7 all-gather.4
  98.4 149.0 all-gather.2
  256.1 67.6 all-reduce.7
  431.1 71.2 all-reduce.5
  505.5 230.4 reduce-scatter.1
where the time goes:
time: 745 us; the launch traced here: 744 us
  waiting for transfers between devices  581 us (78%)
  matrix products  53.9 us (7%)
  local copies, waits for them, and re-layouts  37.8 us (5%)
  blocking collectives  29.4 us (4%)
  other arithmetic  27 us (4%)
  between operations  14 us (2%)
    reduce_scatter x1, waiting for transfers between devices, per_device(): lax.psum_scatter(slab_grad, 'query', scatter_dimension=0, tiled=True)  234 us
    all_gather x1, waiting for transfers between devices, per_device(): lax.all_gather(teacher_entities, 'query', axis=0, tiled=True)  150 us
    all_gather x1, waiting for transfers between devices, per_device(): lax.all_gather(student_entities, 'query', axis=0, tiled=True)  83.7 us
    psum x1, waiting for transfers between devices, per_device(): query_grad = lax.psum(q_grad, 'entity')  69.5 us
    psum x1, waiting for transfers between devices, per_device(): lax.psum(teacher_part.astype(jnp.bfloat16), 'entity').astype(jnp.float32)  43.3 us
    dot_general x4, matrix products, first_pass(): t = jnp.dot(query_teacher, items[0].T, preferred_element_type=jnp.float32)  20.3 us
    unnamed x21, local copies, waits for them, and re-layouts  16.4 us
  transfers between devices with their start and end apart: 5, of which 5 were waited for; matrix products, arithmetic and copies ran while one was open for 4% of the time, Pallas kernels for 0%

commit v1 on v0

--- a/solution.py
+++ b/solution.py
@@ -26,7 +26,10 @@
     student_relations,
 ):
     teacher_slab, student_slab = (
-        lax.all_gather(teacher_entities, "query", axis=0, tiled=True),
+        jnp.concatenate(
+            lax.all_to_all(jnp.stack([teacher_entities] * lax.axis_size("query")), "query", 0, 0),
+            axis=0,
+        ),
         lax.all_gather(student_entities, "query", axis=0, tiled=True),
     )
     slab = teacher_slab.shape[0]

time: 745 us -> 783 us (1.051)
  local copies, waits for them, and re-layouts: 37.8 us -> 52.7 us
  starting transfers between devices: 0.2 us -> 13.6 us
  waiting for transfers between devices: 581 us -> 591 us
    all_gather x1, waiting for transfers between devices: 83.7 us -> 243 us  [per_device(): lax.all_gather(student_entities, 'query', axis=0, tiled=True)]
    all_gather x1 -> x0, waiting for transfers between devices: 150 us -> none  [per_device(): lax.all_gather(teacher_entities, 'query', axis=0, tiled=True)]
    all_to_all x0 -> x1, starting transfers between devices: none -> 13.3 us  [per_device(): lax.all_to_all(jnp.stack([teacher_entities] * lax.axis_size('query')), 'q...]
    all_to_all x0 -> x1, local copies, waits for them, and re-layouts: none -> 11.3 us  [per_device(): lax.all_to_all(jnp.stack([teacher_entities] * lax.axis_size('query')), 'q...]
    unnamed x21 -> x22, local copies, waits for them, and re-layouts: 16.4 us -> 14.7 us
  transfers between devices with their start and end apart: 5 -> 5, of which waited for: 5 -> 4; matrix products, arithmetic and copies ran while one was open for 4% -> 4% of each run, Pallas kernels for 0% -> 0%
where the time goes in v1:
time: 783 us; the launch traced here: 781 us
  waiting for transfers between devices  591 us (75%)
  matrix products  53.9 us (7%)
  local copies, waits for them, and re-layouts  52.7 us (7%)
  blocking collectives  29.3 us (4%)
  other arithmetic  26.3 us (3%)
  between operations  14 us (2%)
  starting transfers between devices  13.6 us (2%)
    all_gather x1, waiting for transfers between devices, per_device(): lax.all_gather(student_entities, 'query', axis=0, tiled=True)  243 us
    reduce_scatter x1, waiting for transfers between devices, per_device(): lax.psum_scatter(slab_grad, 'query', scatter_dimension=0, tiled=True)  233 us
    psum x1, waiting for transfers between devices, per_device(): query_grad = lax.psum(q_grad, 'entity')  69.6 us
    psum x1, waiting for transfers between devices, per_device(): lax.psum(teacher_part.astype(jnp.bfloat16), 'entity').astype(jnp.float32)  43 us
    dot_general x4, matrix products, first_pass(): t = jnp.dot(query_teacher, items[0].T, preferred_element_type=jnp.float32)  20.3 us
  transfers between devices with their start and end apart: 5, of which 4 were waited for; matrix products, arithmetic and copies ran while one was open for 4% of the time, Pallas kernels for 0%

profile of v1, /device:TPU:32, one launch (start us, length us, event | category | flops | bytes accessed | tf_op | source)
XLA Modules:
  0.0 781.1 jit_solution(3545830057601110933)
XLA Ops:
  7.2 5.2 stack.2
  12.4 13.3 %all-to-all-start = ((bf16[32,128,1000]{1,2,0:T(8,128)(2,1)}), bf16[32,128,1000]{1,2,0:T(8,128)(2,1)}, u32[]{:S(2)}, u32[]{:S(2)}) async-start(bf16[32,128,1000]{1,2,0:T(8,128)(2,1)} %stack.2), calls=%async_computation | async-start | bytes 16384000 | tf_op jit(solution)/shard_map/all_to_all | solution.py:30
  25.8 0.7 all-gather.2.cloned.1.call-update
  26.6 243.5 %all-gather.2.cloned.1.call-done = bf16[4096,128]{1,0:T(8,128)(2,1)} async-done(((bf16[128,128]{1,0:T(8,128)(2,1)}), bf16[4096,128]{1,0:T(8,128)(2,1)}) %all-gather.2.cloned.1.call-update) | async-done | bytes 1048592 | tf_op jit(solution)/shard_map/all_gather | solution.py:33
  270.0 2.4 gather_fusion.2
  272.5 0.9 select_convert_fusion.2
  273.3 11.3 %copy.14 = bf16[32,128,1000]{2,1,0:T(8,128)(2,1)} copy(bf16[32,128,1000]{1,2,0:T(8,128)(2,1)} %all-to-all-done) | data formatting | bytes 16384000 | tf_op jit(solution)/shard_map/all_to_all | solution.py:30
  284.7 7.2 gather_fusion
  291.9 1.3 select_convert_fusion
  293.5 12.3 %copy.16 = bf16[4131,1000]{1,0:T(8,128)(2,1)} copy(bf16[4131,1000]{0,1:T(8,128)(2,1)} %param.16) | data formatting | bytes 16524000 | tf_op args[5]
  305.8 8.0 %gather_fusion.1 = bf16[512,1000]{1,0:T(8,128)(2,1)} fusion(bf16[4131,1000]{1,0:T(8,128)(2,1)} %copy.16, s32[1024]{0:T(1024)S(1)} %pad_clamp_fusion), kind=kCustom, calls=%fused_computation.1 | custom fusion | bytes 2050048 | tf_op jit(solution)/shard_map/jit(_take)/gather | solution.py:48
  313.8 1.3 gather_fusion.3
  315.2 0.6 add_convert_fusion.2
  315.8 0.8 select_convert_fusion.3
  316.6 1.4 select_convert_fusion.1
  318.1 43.0 %all-reduce.8.cloned.1.call-done = (bf16[512,1000]{1,0:T(8,128)(2,1)}, bf16[512,128]{1,0:T(8,128)(2,1)}) async-done(((bf16[512,1000]{1,0:T(8,128)(2,1)}, bf16[512,128]{1,0:T(8,128)(2,1)}), (bf16[512,1000]{1,0:T(8,128)(2,1)}, bf16[512,128]{1,0:T(8,128)(2,1)})) %all-reduce.8.cloned.1.call-update) | async-done | bytes 1155088 | tf_op jit(solution)/shard_map/psum | solution.py:43
  361.1 1.5 convert_element_type.33
  362.6 1.0 subtract_convert_fusion.1
  363.7 1.3 pad_maximum_fusion
  365.4 46.0 %while.32 = (s32[]{:T(128)}, f32[512]{0:T(512)S(1)}, f32[512]{0:T(512)}, f32[512]{0:T(512)}, f32[512]{0:T(512)}, /*index=5*/f32[512]{0:T(512)}, bf16[4,1024,1000...) while((s32[]{:T(128)}, f32[512]{0:T(512)S(1)}, ...), condition=%wide.region_8.9_spmd.clone, body=%wide.region_2.8_spmd.clone.sunk | while | flops 1187518464 | bytes 12046677 | solution.py:78
  365.4 5.1 fusion.51
  370.4 2.0 fusion.52
  372.4 0.7 select_maximum_fusion.4
  373.1 0.7 select_maximum_fusion.5
  373.8 2.4 multiply_reduce_fusion.2
  376.3 0.6 copy.36
  376.9 5.1 fusion.51
  381.9 2.0 fusion.52
  383.9 0.7 select_maximum_fusion.4
  384.6 0.7 select_maximum_fusion.5
  385.3 2.4 multiply_reduce_fusion.2
  387.8 0.6 copy.36
  388.4 5.1 fusion.51
  393.4 2.0 fusion.52
  395.4 0.7 select_maximum_fusion.4
  396.1 0.7 select_maximum_fusion.5
  396.8 2.4 multiply_reduce_fusion.2
  399.3 0.6 copy.36
  399.9 5.1 fusion.51
  404.9 2.0 fusion.52
  406.9 0.7 select_maximum_fusion.4
  407.6 0.7 select_maximum_fusion.5
  408.3 2.4 multiply_reduce_fusion.2
  411.4 14.8 %all-reduce.1 = (f32[512]{0:T(512)}, f32[512]{0:T(512)}) all-reduce(f32[512]{0:T(512)} %get-tuple-element.120, f32[512]{0:T(512)S(1)} %get-tuple-element.118), channel_id=1, replica_groups=mesh['query'=32,'entity'=8] {'entity'}, use_global_device_ids=true, to_apply=%region_12.13 | all-reduce | flops 1024 | bytes 8192 | tf_op jit(solution)/shard_map/pmax | solution.py:82
  426.2 0.7 fusion.24
  426.9 14.5 %all-reduce = (f32[512]{0:T(512)S(1)}, f32[512]{0:T(512)}, f32[512]{0:T(512)}) all-reduce(f32[512]{0:T(512)S(1)} %get-tuple-element.261, f32[512]{0:T(512)S(1)} %get-tuple-element.259, f32[512]{0:T(512)S(1)} %get-tuple-element.258), channel_id=1, replica_groups=mesh['query'=32,'entity'=8] {'entity'}, use_global_device_ids=true, to_apply=%region_13.14 | all-reduce | flops 1536 | bytes 12288 | tf_op jit(solution)/shard_map/psum | solution.py:85
  441.4 26.0 %while.33 = (s32[]{:T(128)}, f32[512,128]{1,0:T(8,128)S(1)}, f32[4,1024,128]{2,1,0:T(8,128)}, bf16[4,1024,128]{2,1,0:T(8,128)(2,1)}, bf16[512,128]{1,0:T(8,128)(...) while((s32[]{:T(128)}, f32[512,128]{1,0:T(8,128)S(1)}, ...), condition=%wide.region_15.16_spmd.clone, body=%wide.region_14.15_spmd.clone.sunk | while | flops 1454505984 | bytes 16531671 | solution.py:102
  441.4 3.2 fusion.62
  444.6 1.5 subtract_convert_fusion.4
  446.6 1.2 fusion.63
  447.9 3.2 fusion.62
  451.1 1.5 subtract_convert_fusion.4
  453.1 1.2 fusion.63
  454.4 3.2 fusion.62
  457.6 1.5 subtract_convert_fusion.4
  459.6 1.2 fusion.63
  460.9 3.2 fusion.62
  464.1 1.5 subtract_convert_fusion.4
  466.1 1.2 fusion.63
  467.4 0.7 copy-done.2
  468.7 1.3 log_add_fusion
  469.9 69.6 %all-reduce.6.cloned.1.call-done = f32[512,128]{1,0:T(8,128)} async-done(((f32[512,128]{1,0:T(8,128)}), f32[512,128]{1,0:T(8,128)}) %all-reduce.6.cloned.1.call-update) | async-done | bytes 262160 | tf_op jit(solution)/shard_map/psum | solution.py:105
  539.5 233.4 %reduce-scatter.2.cloned.1.call-done = f32[128,128]{1,0:T(8,128)} async-done(((f32[4096,128]{1,0:T(8,128)}), f32[128,128]{1,0:T(8,128)}) %reduce-scatter.2.cloned.1.call-update) | async-done | bytes 65552 | tf_op jit(solution)/shard_map/reduce_scatter | solution.py:104
  772.9 1.7 copy.48
  (127 shorter events, 4.3 us)
Async XLA Ops:
  7.2 306.7 %copy-start = (bf16[4131,128]{1,0:T(8,128)(2,1)S(1)}, bf16[4131,128]{1,0:T(8,128)(2,1)}, u32[]{:S(2)}) copy-start(bf16[4131,128]{1,0:T(8,128)(2,1)} %param.17) | copy-start | bytes 3172612
  12.4 14.1 %copy-start.15 = (s32[512]{0:T(512)S(1)}, s32[512]{0:T(512)}, u32[]{:S(2)}) copy-start(s32[512]{0:T(512)} %param.11) | copy-start | bytes 6148
  12.4 260.9 %all-to-all-start = ((bf16[32,128,1000]{1,2,0:T(8,128)(2,1)}), bf16[32,128,1000]{1,2,0:T(8,128)(2,1)}, u32[]{:S(2)}, u32[]{:S(2)}) async-start(bf16[32,128,1000]{1,2,0:T(8,128)(2,1)} %stack.2), calls=%async_computation | async-start | bytes 16384000 | tf_op jit(solution)/shard_map/all_to_all | solution.py:30
  25.7 244.3 %all-gather.2.cloned.1.call-start = ((), (), s32[]{:S(2)}) async-start(), calls=%async_computation.2 | async-start | bytes 1081344 | tf_op jit(solution)/shard_map/all_gather | solution.py:33
  26.5 334.6 %all-reduce.8.cloned.1.call-start = ((), (), s32[]{:S(2)}) async-start(), calls=%async_computation.5 | async-start | bytes 2359296 | tf_op jit(solution)/shard_map/psum | solution.py:43
  291.9 1.6 copy-start.13
  293.2 246.3 %all-reduce.6.cloned.1.call-start = ((), (), s32[]{:S(2)}) async-start(), calls=%async_computation.4 | async-start | bytes 524288 | tf_op jit(solution)/shard_map/psum | solution.py:105
  305.8 9.4 %copy-start.14 = (s32[512]{0:T(512)S(1)}, s32[512]{0:T(512)}, u32[]{:S(2)}) copy-start(s32[512]{0:T(512)} %param.13) | copy-start | bytes 6148
  361.1 1.5 copy-start.5
  361.1 1.5 copy-start.12
  363.6 1.3 copy-start.3
  373.8 2.4 copy-start.4
  373.8 2.4 copy-start.6
  373.8 2.4 copy-start.8
  373.8 2.4 copy-start.10
  376.2 0.6 copy-start.7
  376.2 0.6 copy-start.9
  376.3 0.6 copy-start.11
  385.3 2.4 copy-start.4
  385.3 2.4 copy-start.6
  385.3 2.4 copy-start.8
  385.3 2.4 copy-start.10
  387.7 0.6 copy-start.7
  387.8 0.6 copy-start.9
  387.8 0.6 copy-start.11
  396.8 2.4 copy-start.4
  396.8 2.4 copy-start.6
  396.8 2.4 copy-start.8
  396.8 2.4 copy-start.10
  399.2 0.6 copy-start.7
  399.3 0.6 copy-start.9
  399.3 0.6 copy-start.11
  408.3 2.4 copy-start.4
  408.3 2.4 copy-start.6
  408.3 2.4 copy-start.8
  408.3 2.4 copy-start.10
  410.7 0.6 copy-start.7
  410.8 0.6 copy-start.9
  410.8 0.6 copy-start.11
  441.4 3.2 copy-start.1
  441.4 3.2 copy-start.16
  447.9 3.2 copy-start.1
  447.9 3.2 copy-start.16
  454.4 3.2 copy-start.1
  454.4 3.2 copy-start.16
  460.9 3.2 copy-start.1
  460.9 3.2 copy-start.16
  467.4 0.7 copy-start.2
  467.4 1.3 copy-start.17
  467.4 1.3 copy-start.18
  468.1 304.9 %reduce-scatter.2.cloned.1.call-start = ((), (), s32[]{:S(2)}) async-start(), calls=%async_computation.3 | async-start | bytes 2162688 | tf_op jit(solution)/shard_map/reduce_scatter | solution.py:104
Sparse Core Ops, SparseCore 0:
  30.0 240.0 all-gather.1
  293.3 67.7 all-reduce.7
  468.2 71.2 all-reduce.5
  542.6 230.2 reduce-scatter.1
